TPU v7x, 256 devices: a whole 4x4x8 slice. The times are simulated.
256 devices in a mesh: pairs: 256 (over x, y, z, core).
Axes of the slice: x: 4, y: 4, z: 8, core: 2. Of those that a mesh axis runs over, the one named last changes fastest.
Arguments:
- image_feats: bfloat16 [65536, 768], P('pairs'), may hold values from -6 to 6
- text_feats: bfloat16 [65536, 768], P('pairs'), may hold values from -6 to 6
- image_head: bfloat16 [768, 768], replicated, may hold values from -0.0078125 to 0.0078125
- text_head: bfloat16 [768, 768], replicated, may hold values from -0.0078125 to 0.0078125
- logit_scale: float32 [1], replicated, may hold values from 4 to 16
- logit_bias: float32 [1], replicated, may hold values from -6 to -2
- round_offsets: int32 [4], replicated, may hold values from 1 to 255, as said below
Outputs:
- image_grad: bfloat16 [65536, 768], P('pairs')
- text_grad: bfloat16 [65536, 768], P('pairs')
- image_head_grad: float32 [768, 768], replicated
- text_head_grad: float32 [768, 768], replicated
- scalar_grads: float32 [3], replicated
Inputs may be any that keep to these rules, and one draw needn't show every extreme that they name: `round_offsets`: the 4 offsets are distinct; 1 and 256 - 1 are among them.
All inputs are finite; a program needn't handle non-finite values.
Results may differ from a plain program's by a relative error of at most 0.0065.
Values may be sent and summed in bfloat16 or wider, within the bound.
No kernel may reach another device: no remote copies, remote signals or barrier semaphores. Data moves between devices by JAX's collectives and lax.ppermute only.
A program may use at most 128 MiB of HBM per device.

v0:
```python
import jax
import jax.numpy as jnp
from jax import lax
from jax.sharding import PartitionSpec as P

ROUNDS = 4


EPS = 1e-06


def shifted(value, axis, steps):
    count = lax.axis_size(axis)
    pairs = [(source, (source + steps) % count) for source in range(count)]
    return lax.ppermute(value, axis, pairs)


def embed(feats, head):
    proj = jnp.dot(feats, head, preferred_element_type=jnp.float32)
    norms = jnp.sqrt(jnp.sum(proj * proj, axis=-1, keepdims=True) + EPS)
    return (proj / norms, norms)


def score_tile(left, right, scale, bias, own):
    cosine = jnp.dot(left, right.T, preferred_element_type=jnp.float32)
    logit = scale * cosine + bias
    rows = left.shape[0]
    eye = (jnp.arange(rows)[:, None] == jnp.arange(rows)[None, :]).astype(jnp.float32)
    label = 2.0 * eye - 1.0 if own else -jnp.ones_like(logit)
    loss = jnp.sum(jax.nn.softplus(-label * logit))
    dlogit = -label * jax.nn.sigmoid(-label * logit)
    coef = (scale * dlogit).astype(jnp.bfloat16)
    return (loss, jnp.sum(dlogit * cosine), jnp.sum(dlogit), coef)


def backnorm(zhat, norms, grad):
    inner = jnp.sum(zhat * grad, axis=-1, keepdims=True)
    return ((grad - zhat * inner) / norms).astype(jnp.bfloat16)


def relay(values, distance):
    count = lax.axis_size("pairs")
    nbits = count.bit_length() - 1
    for place in range(nbits):
        moved = shifted(values, "pairs", 1 << place)
        values = jnp.where(distance >> place & 1 == 1, moved, values)
    return values


def local(image_feats, text_feats, image_head, text_head, logit_scale, logit_bias, round_offsets):
    scale = logit_scale[0]
    bias = logit_bias[0]
    count = lax.axis_size("pairs")
    total = float(count * image_feats.shape[0])
    zh_img, n_img = embed(image_feats, image_head)
    zh_txt, n_txt = embed(text_feats, text_head)
    z_img = zh_img.astype(jnp.bfloat16)
    z_txt = zh_txt.astype(jnp.bfloat16)
    loss, gscale, gbias, coef = score_tile(z_img, z_txt, scale, bias, True)
    dz_img = jnp.dot(coef, z_txt, preferred_element_type=jnp.float32)
    dz_txt = jnp.dot(coef.T, z_img, preferred_element_type=jnp.float32)
    for turn in range(ROUNDS):
        offset_now = round_offsets[turn]
        forward = jnp.mod(count - offset_now, count)
        received = relay(z_txt, forward)
        part_loss, part_scale, part_bias, coef = score_tile(z_img, received, scale, bias, False)
        dz_img = dz_img + jnp.dot(coef, received, preferred_element_type=jnp.float32)
        back = jnp.dot(coef.T, z_img, preferred_element_type=jnp.float32).astype(jnp.bfloat16)
        back = relay(back, offset_now)
        dz_txt = dz_txt + back.astype(jnp.float32)
        loss = loss + part_loss
        gscale = gscale + part_scale
        gbias = gbias + part_bias
    du_img = backnorm(zh_img, n_img, dz_img)
    du_txt = backnorm(zh_txt, n_txt, dz_txt)
    g_img = jnp.dot(du_img, image_head.T, preferred_element_type=jnp.float32).astype(jnp.bfloat16)
    g_txt = jnp.dot(du_txt, text_head.T, preferred_element_type=jnp.float32).astype(jnp.bfloat16)
    part_wi = jnp.dot(image_feats.T, du_img, preferred_element_type=jnp.float32)
    part_wt = jnp.dot(text_feats.T, du_txt, preferred_element_type=jnp.float32)
    stats = jnp.stack([loss, gscale, gbias])
    sum_wi, sum_wt, sum_stats = lax.psum((part_wi, part_wt, stats), "pairs")
    return (g_img, g_txt, sum_wi / total, sum_wt / total, sum_stats / total)


def solution(mesh):
    placed = (P("pairs", None), P("pairs", None), P(), P(), P(), P(), P())
    return jax.shard_map(
        local,
        mesh=mesh,
        in_specs=placed,
        out_specs=(P("pairs", None), P("pairs", None), P(), P(), P()),
        check_vma=False,
    )
```

profile of v0, /device:TPU:1, one launch (start us, length us, event | category | flops | bytes accessed | tf_op | source)
XLA Modules:
  0.0 1024.5 jit_solution(8518685417179279752)
XLA Ops:
  47.9 9.2 collective-permute-done.8
  57.2 8.3 collective-permute-done.22
  65.6 8.3 collective-permute-done.15
  74.0 8.3 collective-permute-done.1
  83.0 10.4 %collective-permute-done.9 = bf16[256,768]{1,0:T(8,128)(2,1)S(1)} collective-permute-done((bf16[256,768]{1,0:T(8,128)(2,1)S(1)}, bf16[256,768]{1,0:T(8,128)(2,1)S(1)}, u32[]{:S(2)}, u32[]{:S(2)}) %collective-permute-start.9) | collective-permute-done | bytes 393248 | tf_op jit(solution)/shard_map/ppermute | solution.py:15
  93.4 42.9 %collective-permute-start.10 = (bf16[256,768]{1,0:T(8,128)(2,1)S(1)}, bf16[256,768]{1,0:T(8,128)(2,1)S(1)}, u32[]{:S(2)}, u32[]{:S(2)}) collective-permute-start(bf16[256,768]{1,0:T(8,128)(2,1)S(1)} %broadcast_select_fusion.46), channel_id=1, source_target_pairs={{0,8},{1,9},{2,10},{3,11},{4,12},{5,13},{6,14},{7,15},{8,16},{9,17... | collective-permute-start | bytes 1179656 | tf_op jit(solution)/shard_map/ppermute | solution.py:15
  143.3 29.4 %collective-permute-start.3 = (bf16[256,768]{1,0:T(8,128)(2,1)S(1)}, bf16[256,768]{1,0:T(8,128)(2,1)S(1)}, u32[]{:S(2)}, u32[]{:S(2)}) collective-permute-start(bf16[256,768]{1,0:T(8,128)(2,1)S(1)} %broadcast_select_fusion.54), channel_id=1, source_target_pairs={{0,8},{1,9},{2,10},{3,11},{4,12},{5,13},{6,14},{7,15},{8,16},{9,17... | collective-permute-start | bytes 1179656 | tf_op jit(solution)/shard_map/ppermute | solution.py:15
  172.8 8.3 collective-permute-start.11
  212.7 12.0 %collective-permute-start.26 = (bf16[256,768]{1,0:T(8,128)(2,1)S(1)}, bf16[256,768]{1,0:T(8,128)(2,1)S(1)}, u32[]{:S(2)}, u32[]{:S(2)}) collective-permute-start(bf16[256,768]{1,0:T(8,128)(2,1)S(1)} %broadcast_select_fusion.32), channel_id=1, source_target_pairs={{0,32},{1,33},{2,34},{3,35},{4,36},{5,37},{6,38},{7,39},{8,40},{9,... | collective-permute-start | bytes 1179656 | tf_op jit(solution)/shard_map/ppermute | solution.py:15
  253.7 10.1 collective-permute-start.21
  268.0 95.2 %collective-permute-start.37 = (bf16[256,768]{1,0:T(8,128)(2,1)S(1)}, bf16[256,768]{1,0:T(8,128)(2,1)S(1)}, u32[]{:S(2)}, u32[]{:S(2)}) collective-permute-start(bf16[256,768]{1,0:T(8,128)(2,1)S(1)} %convolution_convert_fusion.3), channel_id=1, source_target_pairs={{0,1},{1,2},{2,3},{3,4},{4,5},{5,6},{6,7},{7,8},{8,9},{9,10},{10,1... | collective-permute-start | bytes 1179656 | tf_op jit(solution)/shard_map/ppermute | solution.py:15
  386.0 10.2 collective-permute-done.38
  396.4 8.3 collective-permute-done.54
  405.0 7.8 collective-permute-done.46
  413.3 13.1 %collective-permute-done.30 = bf16[256,768]{1,0:T(8,128)(2,1)S(1)} collective-permute-done((bf16[256,768]{1,0:T(8,128)(2,1)S(1)}, bf16[256,768]{1,0:T(8,128)(2,1)S(1)}, u32[]{:S(2)}, u32[]{:S(2)}) %collective-permute-start.30) | collective-permute-done | bytes 393248 | tf_op jit(solution)/shard_map/ppermute | solution.py:15
  426.5 17.0 %collective-permute-start.31 = (bf16[256,768]{1,0:T(8,128)(2,1)S(1)}, bf16[256,768]{1,0:T(8,128)(2,1)S(1)}, u32[]{:S(2)}, u32[]{:S(2)}) collective-permute-start(bf16[256,768]{1,0:T(8,128)(2,1)S(1)} %broadcast_select_fusion.22), channel_id=1, source_target_pairs={{0,4},{1,5},{2,6},{3,7},{4,8},{5,9},{6,10},{7,11},{8,12},{9,13},{1... | collective-permute-start | bytes 1179656 | tf_op jit(solution)/shard_map/ppermute | solution.py:15
  443.5 8.8 collective-permute-done.39
  452.4 14.2 %collective-permute-start.40 = (bf16[256,768]{1,0:T(8,128)(2,1)S(1)}, bf16[256,768]{1,0:T(8,128)(2,1)S(1)}, u32[]{:S(2)}, u32[]{:S(2)}) collective-permute-start(bf16[256,768]{1,0:T(8,128)(2,1)S(1)} %broadcast_select_fusion.16), channel_id=1, source_target_pairs={{0,8},{1,9},{2,10},{3,11},{4,12},{5,13},{6,14},{7,15},{8,16},{9,17... | collective-permute-start | bytes 1179656 | tf_op jit(solution)/shard_map/ppermute | solution.py:15
  466.6 10.7 %collective-permute-start.56 = (bf16[256,768]{1,0:T(8,128)(2,1)S(1)}, bf16[256,768]{1,0:T(8,128)(2,1)S(1)}, u32[]{:S(2)}, u32[]{:S(2)}) collective-permute-start(bf16[256,768]{1,0:T(8,128)(2,1)S(1)} %broadcast_select_fusion.2), channel_id=1, source_target_pairs={{0,8},{1,9},{2,10},{3,11},{4,12},{5,13},{6,14},{7,15},{8,16},{9,17... | collective-permute-start | bytes 1179656 | tf_op jit(solution)/shard_map/ppermute | solution.py:15
  477.4 9.4 collective-permute-start.48
  486.8 34.6 %collective-permute-start.32 = (bf16[256,768]{1,0:T(8,128)(2,1)S(1)}, bf16[256,768]{1,0:T(8,128)(2,1)S(1)}, u32[]{:S(2)}, u32[]{:S(2)}) collective-permute-start(bf16[256,768]{1,0:T(8,128)(2,1)S(1)} %broadcast_select_fusion.23), channel_id=1, source_target_pairs={{0,8},{1,9},{2,10},{3,11},{4,12},{5,13},{6,14},{7,15},{8,16},{9,17... | collective-permute-start | bytes 1179656 | tf_op jit(solution)/shard_map/ppermute | solution.py:15
  521.5 15.8 %collective-permute-start.41 = (bf16[256,768]{1,0:T(8,128)(2,1)S(1)}, bf16[256,768]{1,0:T(8,128)(2,1)S(1)}, u32[]{:S(2)}, u32[]{:S(2)}) collective-permute-start(bf16[256,768]{1,0:T(8,128)(2,1)S(1)} %broadcast_select_fusion.17), channel_id=1, source_target_pairs={{0,16},{1,17},{2,18},{3,19},{4,20},{5,21},{6,22},{7,23},{8,24},{9,... | collective-permute-start | bytes 1179656 | tf_op jit(solution)/shard_map/ppermute | solution.py:15
  537.3 9.5 collective-permute-start.57
  546.8 19.5 %collective-permute-start.49 = (bf16[256,768]{1,0:T(8,128)(2,1)S(1)}, bf16[256,768]{1,0:T(8,128)(2,1)S(1)}, u32[]{:S(2)}, u32[]{:S(2)}) collective-permute-start(bf16[256,768]{1,0:T(8,128)(2,1)S(1)} %broadcast_select_fusion.10), channel_id=1, source_target_pairs={{0,16},{1,17},{2,18},{3,19},{4,20},{5,21},{6,22},{7,23},{8,24},{9,... | collective-permute-start | bytes 1179656 | tf_op jit(solution)/shard_map/ppermute | solution.py:15
  566.3 8.0 collective-permute-start.33
  574.4 8.6 collective-permute-start.42
  583.0 26.9 %collective-permute-start.58 = (bf16[256,768]{1,0:T(8,128)(2,1)S(1)}, bf16[256,768]{1,0:T(8,128)(2,1)S(1)}, u32[]{:S(2)}, u32[]{:S(2)}) collective-permute-start(bf16[256,768]{1,0:T(8,128)(2,1)S(1)} %broadcast_select_fusion.4), channel_id=1, source_target_pairs={{0,32},{1,33},{2,34},{3,35},{4,36},{5,37},{6,38},{7,39},{8,40},{9,... | collective-permute-start | bytes 1179656 | tf_op jit(solution)/shard_map/ppermute | solution.py:15
  638.8 8.4 collective-permute-start.60
  647.2 29.4 %collective-permute-start.52 = (bf16[256,768]{1,0:T(8,128)(2,1)S(1)}, bf16[256,768]{1,0:T(8,128)(2,1)S(1)}, u32[]{:S(2)}, u32[]{:S(2)}) collective-permute-start(bf16[256,768]{1,0:T(8,128)(2,1)S(1)} %broadcast_select_fusion.13), channel_id=1, source_target_pairs={{0,128},{1,129},{2,130},{3,131},{4,132},{5,133},{6,134},{7,135},{8... | collective-permute-start | bytes 1179656 | tf_op jit(solution)/shard_map/ppermute | solution.py:15
  676.7 13.7 %collective-permute-start.36 = (bf16[256,768]{1,0:T(8,128)(2,1)S(1)}, bf16[256,768]{1,0:T(8,128)(2,1)S(1)}, u32[]{:S(2)}, u32[]{:S(2)}) collective-permute-start(bf16[256,768]{1,0:T(8,128)(2,1)S(1)} %broadcast_select_fusion.27), channel_id=1, source_target_pairs={{0,128},{1,129},{2,130},{3,131},{4,132},{5,133},{6,134},{7,135},{8... | collective-permute-start | bytes 1179656 | tf_op jit(solution)/shard_map/ppermute | solution.py:15
  708.2 116.4 %psum.23 = f32[3]{0:T(128)S(1)} all-reduce(f32[3]{0:T(128)S(1)} %pad_maximum_fusion), channel_id=1, replica_groups=mesh['pairs'=256] {'pairs'}, use_global_device_ids=true, to_apply=%region_21.22 | all-reduce | flops 3 | bytes 24 | tf_op jit(solution)/shard_map/psum | solution.py:81
  827.6 180.6 %all-reduce.3.cloned.1.call-done = (f32[768,768]{0,1:T(8,128)}, f32[768,768]{0,1:T(8,128)}) async-done(((f32[768,768]{0,1:T(8,128)}, f32[768,768]{0,1:T(8,128)}), (f32[768,768]{0,1:T(8,128)}, f32[768,768]{0,1:T(8,128)})) %all-reduce.3.cloned.1.call-update) | async-done | bytes 4718608 | tf_op jit(solution)/shard_map/psum | solution.py:81
  (191 shorter events, 162.0 us)
Async XLA Ops:
  7.2 1001.0 %all-reduce.3.cloned.1.call-start = ((), (), s32[]{:S(2)}) async-start(), calls=%async_computation | async-start | bytes 9437184 | tf_op jit(solution)/shard_map/psum | solution.py:81
  65.5 70.8 %collective-permute-start.23 = (bf16[256,768]{1,0:T(8,128)(2,1)S(1)}, bf16[256,768]{1,0:T(8,128)(2,1)S(1)}, u32[]{:S(2)}, u32[]{:S(2)}) collective-permute-start(bf16[256,768]{1,0:T(8,128)(2,1)S(1)} %broadcast_select_fusion.29), channel_id=1, source_target_pairs={{0,4},{1,5},{2,6},{3,7},{4,8},{5,9},{6,10},{7,11},{8,12},{9,13},{1... | collective-permute-start | bytes 1179656 | tf_op jit(solution)/shard_map/ppermute | solution.py:15
  73.9 62.5 %collective-permute-start.16 = (bf16[256,768]{1,0:T(8,128)(2,1)S(1)}, bf16[256,768]{1,0:T(8,128)(2,1)S(1)}, u32[]{:S(2)}, u32[]{:S(2)}) collective-permute-start(bf16[256,768]{1,0:T(8,128)(2,1)S(1)} %broadcast_select_fusion.37), channel_id=1, source_target_pairs={{0,4},{1,5},{2,6},{3,7},{4,8},{5,9},{6,10},{7,11},{8,12},{9,13},{1... | collective-permute-start | bytes 1179656 | tf_op jit(solution)/shard_map/ppermute | solution.py:15
  82.4 60.9 %collective-permute-start.2 = (bf16[256,768]{1,0:T(8,128)(2,1)S(1)}, bf16[256,768]{1,0:T(8,128)(2,1)S(1)}, u32[]{:S(2)}, u32[]{:S(2)}) collective-permute-start(bf16[256,768]{1,0:T(8,128)(2,1)S(1)} %broadcast_select_fusion.53), channel_id=1, source_target_pairs={{0,4},{1,5},{2,6},{3,7},{4,8},{5,9},{6,10},{7,11},{8,12},{9,13},{1... | collective-permute-start | bytes 1179656 | tf_op jit(solution)/shard_map/ppermute | solution.py:15
  93.4 79.3 %collective-permute-start.10 = (bf16[256,768]{1,0:T(8,128)(2,1)S(1)}, bf16[256,768]{1,0:T(8,128)(2,1)S(1)}, u32[]{:S(2)}, u32[]{:S(2)}) collective-permute-start(bf16[256,768]{1,0:T(8,128)(2,1)S(1)} %broadcast_select_fusion.46), channel_id=1, source_target_pairs={{0,8},{1,9},{2,10},{3,11},{4,12},{5,13},{6,14},{7,15},{8,16},{9,17... | collective-permute-start | bytes 1179656 | tf_op jit(solution)/shard_map/ppermute | solution.py:15
  136.4 44.8 %collective-permute-start.24 = (bf16[256,768]{1,0:T(8,128)(2,1)S(1)}, bf16[256,768]{1,0:T(8,128)(2,1)S(1)}, u32[]{:S(2)}, u32[]{:S(2)}) collective-permute-start(bf16[256,768]{1,0:T(8,128)(2,1)S(1)} %broadcast_select_fusion.30), channel_id=1, source_target_pairs={{0,8},{1,9},{2,10},{3,11},{4,12},{5,13},{6,14},{7,15},{8,16},{9,17... | collective-permute-start | bytes 1179656 | tf_op jit(solution)/shard_map/ppermute | solution.py:15
  136.5 56.8 %collective-permute-start.17 = (bf16[256,768]{1,0:T(8,128)(2,1)S(1)}, bf16[256,768]{1,0:T(8,128)(2,1)S(1)}, u32[]{:S(2)}, u32[]{:S(2)}) collective-permute-start(bf16[256,768]{1,0:T(8,128)(2,1)S(1)} %broadcast_select_fusion.38), channel_id=1, source_target_pairs={{0,8},{1,9},{2,10},{3,11},{4,12},{5,13},{6,14},{7,15},{8,16},{9,17... | collective-permute-start | bytes 1179656 | tf_op jit(solution)/shard_map/ppermute | solution.py:15
  143.3 62.3 %collective-permute-start.3 = (bf16[256,768]{1,0:T(8,128)(2,1)S(1)}, bf16[256,768]{1,0:T(8,128)(2,1)S(1)}, u32[]{:S(2)}, u32[]{:S(2)}) collective-permute-start(bf16[256,768]{1,0:T(8,128)(2,1)S(1)} %broadcast_select_fusion.54), channel_id=1, source_target_pairs={{0,8},{1,9},{2,10},{3,11},{4,12},{5,13},{6,14},{7,15},{8,16},{9,17... | collective-permute-start | bytes 1179656 | tf_op jit(solution)/shard_map/ppermute | solution.py:15
  172.8 39.7 %collective-permute-start.11 = (bf16[256,768]{1,0:T(8,128)(2,1)S(1)}, bf16[256,768]{1,0:T(8,128)(2,1)S(1)}, u32[]{:S(2)}, u32[]{:S(2)}) collective-permute-start(bf16[256,768]{1,0:T(8,128)(2,1)S(1)} %broadcast_select_fusion.47), channel_id=1, source_target_pairs={{0,16},{1,17},{2,18},{3,19},{4,20},{5,21},{6,22},{7,23},{8,24},{9,... | collective-permute-start | bytes 1179656 | tf_op jit(solution)/shard_map/ppermute | solution.py:15
  251.8 111.5 %collective-permute-start.28 = (bf16[256,768]{1,0:T(8,128)(2,1)S(1)}, bf16[256,768]{1,0:T(8,128)(2,1)S(1)}, u32[]{:S(2)}, u32[]{:S(2)}) collective-permute-start(bf16[256,768]{1,0:T(8,128)(2,1)S(1)} %broadcast_select_fusion.34), channel_id=1, source_target_pairs={{0,128},{1,129},{2,130},{3,131},{4,132},{5,133},{6,134},{7,135},{8... | collective-permute-start | bytes 1179656 | tf_op jit(solution)/shard_map/ppermute | solution.py:15
  253.7 111.2 %collective-permute-start.21 = (bf16[256,768]{1,0:T(8,128)(2,1)S(1)}, bf16[256,768]{1,0:T(8,128)(2,1)S(1)}, u32[]{:S(2)}, u32[]{:S(2)}) collective-permute-start(bf16[256,768]{1,0:T(8,128)(2,1)S(1)} %broadcast_select_fusion.42), channel_id=1, source_target_pairs={{0,128},{1,129},{2,130},{3,131},{4,132},{5,133},{6,134},{7,135},{8... | collective-permute-start | bytes 1179656 | tf_op jit(solution)/shard_map/ppermute | solution.py:15
  266.4 100.1 %collective-permute-start.7 = (bf16[256,768]{1,0:T(8,128)(2,1)S(1)}, bf16[256,768]{1,0:T(8,128)(2,1)S(1)}, u32[]{:S(2)}, u32[]{:S(2)}) collective-permute-start(bf16[256,768]{1,0:T(8,128)(2,1)S(1)} %broadcast_select_fusion.58), channel_id=1, source_target_pairs={{0,128},{1,129},{2,130},{3,131},{4,132},{5,133},{6,134},{7,135},{8... | collective-permute-start | bytes 1179656 | tf_op jit(solution)/shard_map/ppermute | solution.py:15
  268.0 102.4 %collective-permute-start.37 = (bf16[256,768]{1,0:T(8,128)(2,1)S(1)}, bf16[256,768]{1,0:T(8,128)(2,1)S(1)}, u32[]{:S(2)}, u32[]{:S(2)}) collective-permute-start(bf16[256,768]{1,0:T(8,128)(2,1)S(1)} %convolution_convert_fusion.3), channel_id=1, source_target_pairs={{0,1},{1,2},{2,3},{3,4},{4,5},{5,6},{6,7},{7,8},{8,9},{9,10},{10,1... | collective-permute-start | bytes 1179656 | tf_op jit(solution)/shard_map/ppermute | solution.py:15
  385.9 40.5 %collective-permute-start.30 = (bf16[256,768]{1,0:T(8,128)(2,1)S(1)}, bf16[256,768]{1,0:T(8,128)(2,1)S(1)}, u32[]{:S(2)}, u32[]{:S(2)}) collective-permute-start(bf16[256,768]{1,0:T(8,128)(2,1)S(1)} %broadcast_select_fusion.21), channel_id=1, source_target_pairs={{0,2},{1,3},{2,4},{3,5},{4,6},{5,7},{6,8},{7,9},{8,10},{9,11},{10,... | collective-permute-start | bytes 1179656 | tf_op jit(solution)/shard_map/ppermute | solution.py:15
  396.3 56.0 %collective-permute-start.39 = (bf16[256,768]{1,0:T(8,128)(2,1)S(1)}, bf16[256,768]{1,0:T(8,128)(2,1)S(1)}, u32[]{:S(2)}, u32[]{:S(2)}) collective-permute-start(bf16[256,768]{1,0:T(8,128)(2,1)S(1)} %broadcast_select_fusion.15), channel_id=1, source_target_pairs={{0,4},{1,5},{2,6},{3,7},{4,8},{5,9},{6,10},{7,11},{8,12},{9,13},{1... | collective-permute-start | bytes 1179656 | tf_op jit(solution)/shard_map/ppermute | solution.py:15
  404.7 61.8 %collective-permute-start.55 = (bf16[256,768]{1,0:T(8,128)(2,1)S(1)}, bf16[256,768]{1,0:T(8,128)(2,1)S(1)}, u32[]{:S(2)}, u32[]{:S(2)}) collective-permute-start(bf16[256,768]{1,0:T(8,128)(2,1)S(1)} %broadcast_select_fusion.1), channel_id=1, source_target_pairs={{0,4},{1,5},{2,6},{3,7},{4,8},{5,9},{6,10},{7,11},{8,12},{9,13},{1... | collective-permute-start | bytes 1179656 | tf_op jit(solution)/shard_map/ppermute | solution.py:15
  412.9 64.4 %collective-permute-start.47 = (bf16[256,768]{1,0:T(8,128)(2,1)S(1)}, bf16[256,768]{1,0:T(8,128)(2,1)S(1)}, u32[]{:S(2)}, u32[]{:S(2)}) collective-permute-start(bf16[256,768]{1,0:T(8,128)(2,1)S(1)} %broadcast_select_fusion.8), channel_id=1, source_target_pairs={{0,4},{1,5},{2,6},{3,7},{4,8},{5,9},{6,10},{7,11},{8,12},{9,13},{1... | collective-permute-start | bytes 1179656 | tf_op jit(solution)/shard_map/ppermute | solution.py:15
  426.5 60.3 %collective-permute-start.31 = (bf16[256,768]{1,0:T(8,128)(2,1)S(1)}, bf16[256,768]{1,0:T(8,128)(2,1)S(1)}, u32[]{:S(2)}, u32[]{:S(2)}) collective-permute-start(bf16[256,768]{1,0:T(8,128)(2,1)S(1)} %broadcast_select_fusion.22), channel_id=1, source_target_pairs={{0,4},{1,5},{2,6},{3,7},{4,8},{5,9},{6,10},{7,11},{8,12},{9,13},{1... | collective-permute-start | bytes 1179656 | tf_op jit(solution)/shard_map/ppermute | solution.py:15
  452.4 69.0 %collective-permute-start.40 = (bf16[256,768]{1,0:T(8,128)(2,1)S(1)}, bf16[256,768]{1,0:T(8,128)(2,1)S(1)}, u32[]{:S(2)}, u32[]{:S(2)}) collective-permute-start(bf16[256,768]{1,0:T(8,128)(2,1)S(1)} %broadcast_select_fusion.16), channel_id=1, source_target_pairs={{0,8},{1,9},{2,10},{3,11},{4,12},{5,13},{6,14},{7,15},{8,16},{9,17... | collective-permute-start | bytes 1179656 | tf_op jit(solution)/shard_map/ppermute | solution.py:15
  466.6 70.6 %collective-permute-start.56 = (bf16[256,768]{1,0:T(8,128)(2,1)S(1)}, bf16[256,768]{1,0:T(8,128)(2,1)S(1)}, u32[]{:S(2)}, u32[]{:S(2)}) collective-permute-start(bf16[256,768]{1,0:T(8,128)(2,1)S(1)} %broadcast_select_fusion.2), channel_id=1, source_target_pairs={{0,8},{1,9},{2,10},{3,11},{4,12},{5,13},{6,14},{7,15},{8,16},{9,17... | collective-permute-start | bytes 1179656 | tf_op jit(solution)/shard_map/ppermute | solution.py:15
  477.4 69.4 %collective-permute-start.48 = (bf16[256,768]{1,0:T(8,128)(2,1)S(1)}, bf16[256,768]{1,0:T(8,128)(2,1)S(1)}, u32[]{:S(2)}, u32[]{:S(2)}) collective-permute-start(bf16[256,768]{1,0:T(8,128)(2,1)S(1)} %broadcast_select_fusion.9), channel_id=1, source_target_pairs={{0,8},{1,9},{2,10},{3,11},{4,12},{5,13},{6,14},{7,15},{8,16},{9,17... | collective-permute-start | bytes 1179656 | tf_op jit(solution)/shard_map/ppermute | solution.py:15
  486.8 79.5 %collective-permute-start.32 = (bf16[256,768]{1,0:T(8,128)(2,1)S(1)}, bf16[256,768]{1,0:T(8,128)(2,1)S(1)}, u32[]{:S(2)}, u32[]{:S(2)}) collective-permute-start(bf16[256,768]{1,0:T(8,128)(2,1)S(1)} %broadcast_select_fusion.23), channel_id=1, source_target_pairs={{0,8},{1,9},{2,10},{3,11},{4,12},{5,13},{6,14},{7,15},{8,16},{9,17... | collective-permute-start | bytes 1179656 | tf_op jit(solution)/shard_map/ppermute | solution.py:15
  521.5 52.9 %collective-permute-start.41 = (bf16[256,768]{1,0:T(8,128)(2,1)S(1)}, bf16[256,768]{1,0:T(8,128)(2,1)S(1)}, u32[]{:S(2)}, u32[]{:S(2)}) collective-permute-start(bf16[256,768]{1,0:T(8,128)(2,1)S(1)} %broadcast_select_fusion.17), channel_id=1, source_target_pairs={{0,16},{1,17},{2,18},{3,19},{4,20},{5,21},{6,22},{7,23},{8,24},{9,... | collective-permute-start | bytes 1179656 | tf_op jit(solution)/shard_map/ppermute | solution.py:15
  537.3 45.7 %collective-permute-start.57 = (bf16[256,768]{1,0:T(8,128)(2,1)S(1)}, bf16[256,768]{1,0:T(8,128)(2,1)S(1)}, u32[]{:S(2)}, u32[]{:S(2)}) collective-permute-start(bf16[256,768]{1,0:T(8,128)(2,1)S(1)} %broadcast_select_fusion.3), channel_id=1, source_target_pairs={{0,16},{1,17},{2,18},{3,19},{4,20},{5,21},{6,22},{7,23},{8,24},{9,... | collective-permute-start | bytes 1179656 | tf_op jit(solution)/shard_map/ppermute | solution.py:15
  546.8 63.1 %collective-permute-start.49 = (bf16[256,768]{1,0:T(8,128)(2,1)S(1)}, bf16[256,768]{1,0:T(8,128)(2,1)S(1)}, u32[]{:S(2)}, u32[]{:S(2)}) collective-permute-start(bf16[256,768]{1,0:T(8,128)(2,1)S(1)} %broadcast_select_fusion.10), channel_id=1, source_target_pairs={{0,16},{1,17},{2,18},{3,19},{4,20},{5,21},{6,22},{7,23},{8,24},{9,... | collective-permute-start | bytes 1179656 | tf_op jit(solution)/shard_map/ppermute | solution.py:15
  566.3 48.1 %collective-permute-start.33 = (bf16[256,768]{1,0:T(8,128)(2,1)S(1)}, bf16[256,768]{1,0:T(8,128)(2,1)S(1)}, u32[]{:S(2)}, u32[]{:S(2)}) collective-permute-start(bf16[256,768]{1,0:T(8,128)(2,1)S(1)} %broadcast_select_fusion.24), channel_id=1, source_target_pairs={{0,16},{1,17},{2,18},{3,19},{4,20},{5,21},{6,22},{7,23},{8,24},{9,... | collective-permute-start | bytes 1179656 | tf_op jit(solution)/shard_map/ppermute | solution.py:15
  574.4 46.9 %collective-permute-start.42 = (bf16[256,768]{1,0:T(8,128)(2,1)S(1)}, bf16[256,768]{1,0:T(8,128)(2,1)S(1)}, u32[]{:S(2)}, u32[]{:S(2)}) collective-permute-start(bf16[256,768]{1,0:T(8,128)(2,1)S(1)} %broadcast_select_fusion.18), channel_id=1, source_target_pairs={{0,32},{1,33},{2,34},{3,35},{4,36},{5,37},{6,38},{7,39},{8,40},{9,... | collective-permute-start | bytes 1179656 | tf_op jit(solution)/shard_map/ppermute | solution.py:15
  583.0 38.4 %collective-permute-start.58 = (bf16[256,768]{1,0:T(8,128)(2,1)S(1)}, bf16[256,768]{1,0:T(8,128)(2,1)S(1)}, u32[]{:S(2)}, u32[]{:S(2)}) collective-permute-start(bf16[256,768]{1,0:T(8,128)(2,1)S(1)} %broadcast_select_fusion.4), channel_id=1, source_target_pairs={{0,32},{1,33},{2,34},{3,35},{4,36},{5,37},{6,38},{7,39},{8,40},{9,... | collective-permute-start | bytes 1179656 | tf_op jit(solution)/shard_map/ppermute | solution.py:15
  633.0 43.6 %collective-permute-start.35 = (bf16[256,768]{1,0:T(8,128)(2,1)S(1)}, bf16[256,768]{1,0:T(8,128)(2,1)S(1)}, u32[]{:S(2)}, u32[]{:S(2)}) collective-permute-start(bf16[256,768]{1,0:T(8,128)(2,1)S(1)} %broadcast_select_fusion.26), channel_id=1, source_target_pairs={{0,64},{1,65},{2,66},{3,67},{4,68},{5,69},{6,70},{7,71},{8,72},{9,... | collective-permute-start | bytes 1179656 | tf_op jit(solution)/shard_map/ppermute | solution.py:15
  637.9 54.6 %collective-permute-start.44 = (bf16[256,768]{1,0:T(8,128)(2,1)S(1)}, bf16[256,768]{1,0:T(8,128)(2,1)S(1)}, u32[]{:S(2)}, u32[]{:S(2)}) collective-permute-start(bf16[256,768]{1,0:T(8,128)(2,1)S(1)} %broadcast_select_fusion.20), channel_id=1, source_target_pairs={{0,128},{1,129},{2,130},{3,131},{4,132},{5,133},{6,134},{7,135},{8... | collective-permute-start | bytes 1179656 | tf_op jit(solution)/shard_map/ppermute | solution.py:15
  638.8 53.8 %collective-permute-start.60 = (bf16[256,768]{1,0:T(8,128)(2,1)S(1)}, bf16[256,768]{1,0:T(8,128)(2,1)S(1)}, u32[]{:S(2)}, u32[]{:S(2)}) collective-permute-start(bf16[256,768]{1,0:T(8,128)(2,1)S(1)} %broadcast_select_fusion.6), channel_id=1, source_target_pairs={{0,128},{1,129},{2,130},{3,131},{4,132},{5,133},{6,134},{7,135},{8... | collective-permute-start | bytes 1179656 | tf_op jit(solution)/shard_map/ppermute | solution.py:15
  647.2 45.4 %collective-permute-start.52 = (bf16[256,768]{1,0:T(8,128)(2,1)S(1)}, bf16[256,768]{1,0:T(8,128)(2,1)S(1)}, u32[]{:S(2)}, u32[]{:S(2)}) collective-permute-start(bf16[256,768]{1,0:T(8,128)(2,1)S(1)} %broadcast_select_fusion.13), channel_id=1, source_target_pairs={{0,128},{1,129},{2,130},{3,131},{4,132},{5,133},{6,134},{7,135},{8... | collective-permute-start | bytes 1179656 | tf_op jit(solution)/shard_map/ppermute | solution.py:15
  (35 other events, 850.5 us)
Sparse Core Ops, SparseCore 0:
  698.6 309.4 all-reduce.2
where the time goes:
time: 1030 us; the launch traced here: 1020 us
  starting transfers between devices  503 us (49%)
  waiting for transfers between devices  323 us (31%)
  blocking collectives  116 us (11%)
  between operations  49.4 us (5%)
  matrix products  18.5 us (2%)
    ppermute x61, starting transfers between devices, shifted(): return lax.ppermute(value, axis, pairs)  503 us
    psum x1, waiting for transfers between devices, local(): sum_wi, sum_wt, sum_stats = lax.psum((part_wi, part_wt, stats), 'pairs')  181 us
    ppermute x61, waiting for transfers between devices, shifted(): return lax.ppermute(value, axis, pairs)  142 us
    psum x1, blocking collectives, local(): sum_wi, sum_wt, sum_stats = lax.psum((part_wi, part_wt, stats), 'pairs')  116 us
  transfers between devices with their start and end apart: 62, of which 24 were waited for; matrix products, arithmetic and copies ran while one was open for 2% of the time, Pallas kernels for 0%

commit v1 on v0

v1 whole, which is shorter than its diff:
```python
import jax
import jax.numpy as jnp
from jax import lax
from jax.experimental import pallas as pl
from jax.experimental.pallas import tpu as pltpu
from jax.sharding import PartitionSpec as P

EPS = 1e-06
X, Y, Z, CORES = 4, 4, 8, 2
COUNT = X * Y * Z * CORES
STEP = Z * CORES
HALF = STEP // 2

PLANES = [[xy * STEP + zc for xy in range(X * Y)] for zc in range(STEP)]
COLUMNS = [[xy * STEP + z * CORES + c for z in range(Z)] for xy in range(X * Y) for c in range(CORES)]


def shifted(value, steps):
    return lax.ppermute(value, "pairs", [(source, (source + steps) % COUNT) for source in range(COUNT)])


def other_core(value):
    return lax.ppermute(value, "pairs", [(source, source ^ 1) for source in range(COUNT)])


def exchange(value, groups):
    return lax.all_to_all(value, "pairs", 0, 0, axis_index_groups=groups, tiled=True)


def embed_kernel(xi_ref, xt_ref, wi_ref, wt_ref, zi_ref, zt_ref, both_ref, zh_ref, n_ref):
    for k, (x_ref, w_ref, z_ref) in enumerate(((xi_ref, wi_ref, zi_ref), (xt_ref, wt_ref, zt_ref))):
        rows = x_ref.shape[0]
        at = slice(k * rows, (k + 1) * rows)
        proj = jnp.dot(x_ref[...], w_ref[...], preferred_element_type=jnp.float32)
        norms = jnp.sqrt(jnp.sum(proj * proj, axis=-1, keepdims=True) + EPS)
        zh = proj / norms
        z = zh.astype(jnp.bfloat16)
        n_ref[at, :] = norms
        zh_ref[at, :] = zh
        z_ref[...] = z
        both_ref[at, :] = z


def embed(image_feats, text_feats, image_head, text_head):
    rows, width = image_feats.shape
    vmem = pl.BlockSpec(memory_space=pltpu.VMEM)
    return pl.pallas_call(
        embed_kernel,
        out_shape=(
            jax.ShapeDtypeStruct((rows, width), jnp.bfloat16),
            jax.ShapeDtypeStruct((rows, width), jnp.bfloat16),
            jax.ShapeDtypeStruct((2 * rows, width), jnp.bfloat16),
            jax.ShapeDtypeStruct((2 * rows, width), jnp.float32),
            jax.ShapeDtypeStruct((2 * rows, 1), jnp.float32),
        ),
        in_specs=[vmem] * 4,
        out_specs=(vmem,) * 5,
        compiler_params=pltpu.CompilerParams(vmem_limit_bytes=32 * 1024 * 1024),
        name="embed",
    )(image_feats, text_feats, image_head, text_head)


def swap(z_img, z_txt, offset):
    low = jnp.mod(offset + HALF, STEP)
    high = jnp.mod((offset + HALF) // STEP, COUNT // STEP)

    def branch(steps):
        if steps == 0:
            return lambda txt, img: (txt, img)
        return lambda txt, img: (shifted(txt, -steps), shifted(img, steps))

    txt, img = lax.switch(low, [branch(k - HALF) for k in range(STEP)], z_txt, z_img)
    return tuple(lax.switch(high, [branch(k * STEP) for k in range(COUNT // STEP)], txt, img))


def dot_t(left, right):
    return lax.dot_general(left, right, (((1,), (1,)), ((), ())), preferred_element_type=jnp.float32)


def tiles_kernel(sb_ref, core_ref, zi_ref, zt_ref, zh_ref, n_ref, ahead_ref, behind_ref, t3_ref, i3_ref, t4_ref, i4_ref,
                 xi_ref, xt_ref, dui_ref, dut_ref, kept_ref, given_ref):
    scale = sb_ref[0]
    bias = sb_ref[1]
    zi = zi_ref[...]
    zt = zt_ref[...]
    rows = zi.shape[0]
    own = lax.broadcasted_iota(jnp.int32, (rows, rows), 0) == lax.broadcasted_iota(jnp.int32, (rows, rows), 1)

    def gate(cosine, mine):
        logit = scale * cosine + bias
        v = jnp.where(own, -logit, logit) if mine else logit
        e = jnp.exp(-jnp.abs(v))
        inv = 1.0 / (1.0 + e)
        dlogit = jnp.where(v >= 0, inv, e * inv)
        if mine:
            dlogit = jnp.where(own, -dlogit, dlogit)
        return v, e, dlogit

    def fold(x):
        return jnp.sum(x.reshape(rows // 8, 8, rows), axis=0)

    loss = gscale = gbias = None
    dz_img = dz_txt = None
    images, texts = slice(0, rows), slice(rows, 2 * rows)
    pairs = (
        (lambda: zt, lambda: zi),
        (lambda: ahead_ref[texts, :], lambda: behind_ref[images, :]),
        (lambda: behind_ref[texts, :], lambda: ahead_ref[images, :]),
        (lambda: t3_ref[...], lambda: i3_ref[...]),
        (lambda: t4_ref[...], lambda: i4_ref[...]),
    )
    for k, (get_txt, get_img) in enumerate(pairs):
        txt = get_txt()
        cosine = dot_t(zi, txt)
        v, e, dlogit = gate(cosine, k == 0)
        parts = fold(jnp.maximum(v, 0.0) + jnp.log1p(e)), fold(dlogit * cosine), fold(dlogit)
        coef = (scale * dlogit).astype(jnp.bfloat16)
        to_img = jnp.dot(coef, txt, preferred_element_type=jnp.float32)
        img = get_img()
        if k == 0:
            coef_back = coef.T
        else:
            coef_back = (scale * gate(dot_t(zt, img), False)[2]).astype(jnp.bfloat16)
        to_txt = jnp.dot(coef_back, img, preferred_element_type=jnp.float32)
        if k == 0:
            loss, gscale, gbias = parts
            dz_img, dz_txt = to_img, to_txt
        else:
            loss, gscale, gbias = loss + parts[0], gscale + parts[1], gbias + parts[2]
            dz_img, dz_txt = dz_img + to_img, dz_txt + to_txt

    for dz, at, du_ref in ((dz_img, images, dui_ref), (dz_txt, texts, dut_ref)):
        zh = zh_ref[at, :]
        inner = jnp.sum(zh * dz, axis=-1, keepdims=True)
        du_ref[...] = ((dz - zh * inner) / n_ref[at, :]).astype(jnp.bfloat16)

    def head_grad(out_ref, x_ref, du_ref):
        width = x_ref.shape[1]
        out_ref[0:width, :] = lax.dot_general(
            x_ref[...], du_ref[...], (((0,), (0,)), ((), ())), preferred_element_type=jnp.float32
        )

    core = core_ref[0]

    @pl.when(core == 0)
    def _():
        head_grad(given_ref, xt_ref, dut_ref)
        head_grad(kept_ref, xi_ref, dui_ref)

    @pl.when(core == 1)
    def _():
        head_grad(given_ref, xi_ref, dui_ref)
        head_grad(kept_ref, xt_ref, dut_ref)

    at = lax.broadcasted_iota(jnp.int32, (8, kept_ref.shape[1]), 1)
    stats = jnp.where(at == 0, jnp.sum(loss), jnp.where(at == 1, jnp.sum(gscale), jnp.sum(gbias)))
    stats = jnp.where(at < 3, stats, 0.0)
    last = slice(kept_ref.shape[0] - 8, kept_ref.shape[0])
    kept_ref[last, :] = stats
    given_ref[last, :] = stats


def tiles(sb, core, z_img, z_txt, *others):
    rows, width = z_img.shape
    vmem = pl.BlockSpec(memory_space=pltpu.VMEM)
    return pl.pallas_call(
        tiles_kernel,
        out_shape=(
            jax.ShapeDtypeStruct((rows, width), jnp.bfloat16),
            jax.ShapeDtypeStruct((rows, width), jnp.bfloat16),
            jax.ShapeDtypeStruct((width + 8, width), jnp.float32),
            jax.ShapeDtypeStruct((width + 8, width), jnp.float32),
        ),
        in_specs=[pl.BlockSpec(memory_space=pltpu.SMEM)] * 2 + [vmem] * (2 + len(others)),
        out_specs=(vmem, vmem, vmem, vmem),
        compiler_params=pltpu.CompilerParams(vmem_limit_bytes=40 * 1024 * 1024),
        name="tiles",
    )(sb, core, z_img, z_txt, *others)


def summed_heads(given, kept, total):
    width = kept.shape[1]
    rows = width // (X * Y)
    both = kept + other_core(given)
    part = both[:width].astype(jnp.bfloat16)
    stats = both[width, 0:3]
    one = lax.reduce_precision(stats, 8, 7)
    two = lax.reduce_precision(stats - one, 8, 7)
    three = stats - one - two
    terms = jnp.stack([one, two, three])
    extra = jnp.zeros((8, width), jnp.bfloat16).at[0:3, 0:3].set(terms.astype(jnp.bfloat16))
    plane = jnp.concatenate([part.reshape(X * Y, rows, width), jnp.broadcast_to(extra[None], (X * Y, 8, width))], axis=1)
    plane = exchange(plane, PLANES)
    plane = jnp.sum(plane.astype(jnp.float32), axis=0)
    stats = jnp.sum(plane[rows : rows + 3, 0:3], axis=0)
    few = rows // Z
    extra = jnp.zeros((8 - few, width), jnp.float32).at[0, 0:3].set(stats)
    column = jnp.concatenate([plane[:rows].reshape(Z, few, width), jnp.broadcast_to(extra[None], (Z, 8 - few, width))], axis=1)
    column = jnp.sum(exchange(column, COLUMNS), axis=0) / total
    stats = column[few, 0:3]
    part = column[:few].astype(jnp.bfloat16)
    part = exchange(jnp.broadcast_to(part[None], (Z, few, width)), COLUMNS).reshape(rows, width)
    part = exchange(jnp.broadcast_to(part[None], (X * Y, rows, width)), PLANES).reshape(width, width)
    return part, stats


def local(image_feats, text_feats, image_head, text_head, logit_scale, logit_bias, round_offsets):
    total = float(COUNT * image_feats.shape[0])
    z_img, z_txt, both, zh, norms = embed(image_feats, text_feats, image_head, text_head)
    order = jnp.sort(round_offsets)
    ahead = shifted(both, -1)
    behind = shifted(both, 1)
    far = swap(z_img, z_txt, order[1]) + swap(z_img, z_txt, order[2])
    sb = jnp.concatenate([logit_scale, logit_bias])
    core = lax.axis_index("pairs") % CORES
    du_img, du_txt, kept, given = tiles(
        sb, core.reshape(1), z_img, z_txt, zh, norms, ahead, behind, *far, image_feats, text_feats
    )
    part, sum_stats = summed_heads(given, kept, total)
    first = core == 0
    theirs = other_core(part)
    sum_wi = jnp.where(first, part, theirs).astype(jnp.float32)
    sum_wt = jnp.where(first, theirs, part).astype(jnp.float32)

    g_img = jnp.dot(du_img, image_head.T, preferred_element_type=jnp.float32).astype(jnp.bfloat16)
    g_txt = jnp.dot(du_txt, text_head.T, preferred_element_type=jnp.float32).astype(jnp.bfloat16)
    return (g_img, g_txt, sum_wi, sum_wt, sum_stats)


def solution(mesh):
    placed = (P("pairs", None), P("pairs", None), P(), P(), P(), P(), P())
    return jax.shard_map(
        local,
        mesh=mesh,
        in_specs=placed,
        out_specs=(P("pairs", None), P("pairs", None), P(), P(), P()),
        check_vma=False,
    )
```

time: 1030 us -> 275 us (0.27)
  starting transfers between devices: 503 us -> 44.5 us
  waiting for transfers between devices: 323 us -> 93.3 us
  between operations: 49.4 us -> 3.98 us
  blocking collectives: 116 us -> 75.1 us
  loops' own time: 0 us -> 32.9 us
  matrix products: 18.5 us -> 2.5 us
    ppermute x61 -> x12, starting transfers between devices: 503 us -> 44.5 us  [the longest x10 37.2 us: shifted(): lax.ppermute(value, 'pairs', [(source, (source + steps) % COUNT) for sour...]
    psum x1 -> x0, waiting for transfers between devices: 181 us -> none  [local(): sum_wi, sum_wt, sum_stats = lax.psum((part_wi, part_wt, stats), 'pairs')]
    psum x1 -> x0, blocking collectives: 116 us -> none  [local(): sum_wi, sum_wt, sum_stats = lax.psum((part_wi, part_wt, stats), 'pairs')]
    all_to_all x0 -> x4, blocking collectives: none -> 75.1 us  [exchange(): lax.all_to_all(value, 'pairs', 0, 0, axis_index_groups=groups, tiled=True)]
    ppermute x61 -> x12, waiting for transfers between devices: 142 us -> 93.3 us  [the longest x10 89.1 us: shifted(): lax.ppermute(value, 'pairs', [(source, (source + steps) % COUNT) for sour...]
    another operation x0 -> x4, loops' own time: none -> 32.9 us  [the longest x2 21.2 us: swap(): lax.switch(high, [branch(k * STEP) for k in range(COUNT // STEP)], txt, img)]
    dot_general x19 -> x0, matrix products: 16 us -> none  [the longest x5 5.95 us: score_tile(): cosine = jnp.dot(left, right.T, preferred_element_type=jnp.float32)]
  transfers between devices with their start and end apart: 62 -> 12, of which waited for: 24 -> 8; matrix products, arithmetic and copies ran while one was open for 2% -> 3% of each run, Pallas kernels for 0% -> 0%
where the time goes in v1:
time: 275 us; the launch traced here: 277 us
  waiting for transfers between devices  93.3 us (34%)
  blocking collectives  75.1 us (27%)
  starting transfers between devices  44.5 us (16%)
  loops' own time  32.9 us (12%)
  local copies, waits for them, and re-layouts  10.6 us (4%)
  Pallas kernels  8.75 us (3%)
  other arithmetic  5.61 us (2%)
  between operations  3.98 us (1%)
    ppermute x10, waiting for transfers between devices, shifted(): lax.ppermute(value, 'pairs', [(source, (source + steps) % COUNT) for sour...  89.1 us
    all_to_all x4, blocking collectives, exchange(): lax.all_to_all(value, 'pairs', 0, 0, axis_index_groups=groups, tiled=True)  75.1 us
    ppermute x10, starting transfers between devices, shifted(): lax.ppermute(value, 'pairs', [(source, (source + steps) % COUNT) for sour...  37.2 us
    another operation x2, loops' own time, swap(): lax.switch(high, [branch(k * STEP) for k in range(COUNT // STEP)], txt, img)  21.2 us
    another operation x2, loops' own time, swap(): lax.switch(low, [branch(k - HALF) for k in range(STEP)], z_txt, z_img)  11.7 us
    ppermute x2, starting transfers between devices, other_core(): lax.ppermute(value, 'pairs', [(source, source ^ 1) for source in range(CO...  7.33 us
    pallas_call x1, Pallas kernels, tiles(): pl.pallas_call(tiles_kernel, out_shape=(jax.ShapeDtypeStruct((rows, width...  6.69 us
    unnamed x26, local copies, waits for them, and re-layouts  6.21 us
  transfers between devices with their start and end apart: 12, of which 8 were waited for; matrix products, arithmetic and copies ran while one was open for 3% of the time, Pallas kernels for 0%

profile of v1, /device:TPU:1, one launch (start us, length us, event | category | flops | bytes accessed | tf_op | source)
XLA Modules:
  0.0 277.4 jit_solution(10894418629984188045)
XLA Ops:
  0.6 1.3 copy-done
  1.9 1.3 copy-done.2
  5.2 2.1 embed.1
  7.9 13.8 %collective-permute-start.120 = (bf16[512,768]{1,0:T(8,128)(2,1)}, bf16[512,768]{1,0:T(8,128)(2,1)S(1)}, u32[]{:S(2)}, u32[]{:S(2)}) collective-permute-start(bf16[512,768]{1,0:T(8,128)(2,1)} %get-tuple-element.424), channel_id=1, source_target_pairs={{0,255},{1,0},{2,1},{3,2},{4,3},{5,4},{6,5},{7,6},{8,7},{9,8},{10,... | collective-permute-start | bytes 2359304 | tf_op jit(solution)/shard_map/ppermute | solution.py:19
  21.7 1.8 collective-permute-start.121
  26.2 40.2 %conditional.6 = (bf16[256,768]{1,0:T(8,128)(2,1)}, bf16[256,768]{1,0:T(8,128)(2,1)}) conditional(s32[]{:T(128)} %clamp.15, (bf16[256,768]{1,0:T(8,128)(2,1)}, bf16[256,768]{1,0:T(8,128)(2,1)}) %tuple.236, (bf16[256,768]{1,0:T(8,128)(2,1)}, bf16[256,768]{1,0:T(8,128)(2,1)}) %tuple.236, (bf16[256,768]{1,0:T(8,128)(2,1)}, ...), branch_computations={%region_33.34_spmd, %region_34.35_spmd, %region_35.36_spmd, %regio... | conditional | bytes 3145824 | solution.py:72
  26.2 5.1 %collective-permute-start.64 = (bf16[256,768]{1,0:T(8,128)(2,1)}, bf16[256,768]{1,0:T(8,128)(2,1)}, u32[]{:S(2)}, u32[]{:S(2)}) collective-permute-start(bf16[256,768]{1,0:T(8,128)(2,1)} %get-tuple-element.345), channel_id=1, source_target_pairs={{0,6},{1,7},{2,8},{3,9},{4,10},{5,11},{6,12},{7,13},{8,14},{9,15},... | collective-permute-start | bytes 1179656 | tf_op jit(solution)/shard_map/cond/branch_2_fun/ppermute | solution.py:19
  31.3 4.2 %collective-permute-start.65 = (bf16[256,768]{1,0:T(8,128)(2,1)}, bf16[256,768]{1,0:T(8,128)(2,1)}, u32[]{:S(2)}, u32[]{:S(2)}) collective-permute-start(bf16[256,768]{1,0:T(8,128)(2,1)} %get-tuple-element.346), channel_id=1, source_target_pairs={{0,250},{1,251},{2,252},{3,253},{4,254},{5,255},{6,0},{7,1},{8,2},... | collective-permute-start | bytes 1179656 | tf_op jit(solution)/shard_map/cond/branch_2_fun/ppermute | solution.py:19
  35.5 30.7 %collective-permute-done.64 = bf16[256,768]{1,0:T(8,128)(2,1)} collective-permute-done((bf16[256,768]{1,0:T(8,128)(2,1)}, bf16[256,768]{1,0:T(8,128)(2,1)}, u32[]{:S(2)}, u32[]{:S(2)}) %collective-permute-start.64) | collective-permute-done | bytes 393248 | tf_op jit(solution)/shard_map/cond/branch_2_fun/ppermute | solution.py:19
  66.4 44.7 %conditional.4 = (bf16[256,768]{1,0:T(8,128)(2,1)}, bf16[256,768]{1,0:T(8,128)(2,1)}) conditional(s32[]{:T(128)} %clamp.13, (bf16[256,768]{1,0:T(8,128)(2,1)}, bf16[256,768]{1,0:T(8,128)(2,1)}) %tuple.236, (bf16[256,768]{1,0:T(8,128)(2,1)}, bf16[256,768]{1,0:T(8,128)(2,1)}) %tuple.236, (bf16[256,768]{1,0:T(8,128)(2,1)}, ...), branch_computations={%region_1.2_spmd, %region_2.3_spmd, %region_3.4_spmd, %region_4.5_... | conditional | bytes 3145824 | solution.py:72
  77.9 4.5 %collective-permute-start.26 = (bf16[256,768]{1,0:T(8,128)(2,1)}, bf16[256,768]{1,0:T(8,128)(2,1)}, u32[]{:S(2)}, u32[]{:S(2)}) collective-permute-start(bf16[256,768]{1,0:T(8,128)(2,1)} %get-tuple-element.307), channel_id=1, source_target_pairs={{0,250},{1,251},{2,252},{3,253},{4,254},{5,255},{6,0},{7,1},{8,2},... | collective-permute-start | bytes 1179656 | tf_op jit(solution)/shard_map/cond/branch_14_fun/ppermute | solution.py:19
  82.3 24.0 %collective-permute-done.26 = bf16[256,768]{1,0:T(8,128)(2,1)} collective-permute-done((bf16[256,768]{1,0:T(8,128)(2,1)}, bf16[256,768]{1,0:T(8,128)(2,1)}, u32[]{:S(2)}, u32[]{:S(2)}) %collective-permute-start.26) | collective-permute-done | bytes 393248 | tf_op jit(solution)/shard_map/cond/branch_14_fun/ppermute | solution.py:19
  106.4 4.7 %collective-permute-done.27 = bf16[256,768]{1,0:T(8,128)(2,1)} collective-permute-done((bf16[256,768]{1,0:T(8,128)(2,1)}, bf16[256,768]{1,0:T(8,128)(2,1)}, u32[]{:S(2)}, u32[]{:S(2)}) %collective-permute-start.27) | collective-permute-done | bytes 393248 | tf_op jit(solution)/shard_map/cond/branch_14_fun/ppermute | solution.py:19
  112.4 33.0 %conditional.7 = ((bf16[256,768]{1,0:T(8,128)(2,1)}, bf16[256,768]{1,0:T(8,128)(2,1)})) conditional(s32[]{:T(128)} %clamp.14, (bf16[256,768]{1,0:T(8,128)(2,1)}, bf16[256,768]{1,0:T(8,128)(2,1)}) %conditional.6, (bf16[256,768]{1,0:T(8,128)(2,1)}, bf16[256,768]{1,0:T(8,128)(2,1)}) %conditional.6, ...), branch_computations={%region_49.50_spmd, %region_50.51_spmd, %region_51.52_spmd, %regio... | conditional | bytes 4718696 | solution.py:73
  121.9 5.4 %collective-permute-start.109 = (bf16[256,768]{1,0:T(8,128)(2,1)}, bf16[256,768]{1,0:T(8,128)(2,1)S(1)}, u32[]{:S(2)}, u32[]{:S(2)}) collective-permute-start(bf16[256,768]{1,0:T(8,128)(2,1)} %get-tuple-element.390), channel_id=1, source_target_pairs={{0,160},{1,161},{2,162},{3,163},{4,164},{5,165},{6,166},{7,167},{8... | collective-permute-start | bytes 1179656 | tf_op jit(solution)/shard_map/cond/branch_10_fun/ppermute | solution.py:19
  127.2 8.9 %collective-permute-done.108 = bf16[256,768]{1,0:T(8,128)(2,1)S(1)} collective-permute-done((bf16[256,768]{1,0:T(8,128)(2,1)}, bf16[256,768]{1,0:T(8,128)(2,1)S(1)}, u32[]{:S(2)}, u32[]{:S(2)}) %collective-permute-start.108) | collective-permute-done | bytes 393248 | tf_op jit(solution)/shard_map/cond/branch_10_fun/ppermute | solution.py:19
  136.9 7.7 %collective-permute-done.109 = bf16[256,768]{1,0:T(8,128)(2,1)S(1)} collective-permute-done((bf16[256,768]{1,0:T(8,128)(2,1)}, bf16[256,768]{1,0:T(8,128)(2,1)S(1)}, u32[]{:S(2)}, u32[]{:S(2)}) %collective-permute-start.109) | collective-permute-done | bytes 393248 | tf_op jit(solution)/shard_map/cond/branch_10_fun/ppermute | solution.py:19
  145.4 28.8 %conditional.5 = ((bf16[256,768]{1,0:T(8,128)(2,1)}, bf16[256,768]{1,0:T(8,128)(2,1)})) conditional(s32[]{:T(128)} %clamp.12, (bf16[256,768]{1,0:T(8,128)(2,1)}, bf16[256,768]{1,0:T(8,128)(2,1)}) %conditional.4, (bf16[256,768]{1,0:T(8,128)(2,1)}, bf16[256,768]{1,0:T(8,128)(2,1)}) %conditional.4, ...), branch_computations={%region_17.18_spmd, %region_18.19_spmd, %region_19.20_spmd, %regio... | conditional | bytes 4718696 | solution.py:73
  150.5 2.4 collective-permute-start.39
  152.9 8.1 %collective-permute-done.38 = bf16[256,768]{1,0:T(8,128)(2,1)S(1)} collective-permute-done((bf16[256,768]{1,0:T(8,128)(2,1)}, bf16[256,768]{1,0:T(8,128)(2,1)S(1)}, u32[]{:S(2)}, u32[]{:S(2)}) %collective-permute-start.38) | collective-permute-done | bytes 393248 | tf_op jit(solution)/shard_map/cond/branch_5_fun/ppermute | solution.py:19
  161.7 5.0 %collective-permute-done.39 = bf16[256,768]{1,0:T(8,128)(2,1)S(1)} collective-permute-done((bf16[256,768]{1,0:T(8,128)(2,1)}, bf16[256,768]{1,0:T(8,128)(2,1)S(1)}, u32[]{:S(2)}, u32[]{:S(2)}) %collective-permute-start.39) | collective-permute-done | bytes 393248 | tf_op jit(solution)/shard_map/cond/branch_5_fun/ppermute | solution.py:19
  175.3 6.7 %tiles.1 = (bf16[256,768]{1,0:T(8,128)(2,1)S(1)}, bf16[256,768]{1,0:T(8,128)(2,1)S(1)}, f32[776,768]{1,0:T(8,128)S(1)}, f32[776,768]{1,0:T(8,128)S(1)}) custom-call(f32[2]{0:T(128)S(1)} %pad_maximum_fusion.2.sb_ref, s32[1]{0:T(128)} %bitcast.core_ref, bf16[256,768]{1,0:T(8,128)(2,1)} %get-tuple-element.420.zi_ref, ...), custom_call_target="tpu_custom_call" | custom-call | tf_op jit(solution)/shard_map/tiles/pallas_call | solution.py:166
  182.0 2.0 collective-permute-start.122
  184.0 4.2 %collective-permute-done.122 = f32[776,768]{1,0:T(8,128)S(1)} collective-permute-done((f32[776,768]{1,0:T(8,128)S(1)}, f32[776,768]{1,0:T(8,128)S(1)}, u32[]{:S(2)}, u32[]{:S(2)}) %collective-permute-start.122) | collective-permute-done | bytes 2383904 | tf_op jit(solution)/shard_map/ppermute | solution.py:23
  188.8 25.1 %all_to_all.20 = bf16[16,56,768]{2,1,0:T(8,128)(2,1)S(1)} all-to-all(bf16[16,56,768]{2,1,0:T(8,128)(2,1)S(1)} %pad_maximum_fusion), channel_id=1, replica_groups={{0,16,32,48,64,80,96,112,128,144,160,176,192,208,224,240},{1,17,33,49,6..., dimensions={0} | all-to-all | bytes 2752512 | tf_op jit(solution)/shard_map/all_to_all | solution.py:27
  214.3 22.0 %all_to_all.21 = f32[8,8,768]{2,1,0:T(8,128)S(1)} all-to-all(f32[8,8,768]{2,1,0:T(8,128)S(1)} %pad_maximum_fusion.1), channel_id=1, replica_groups={{0,2,4,6,8,10,12,14},{1,3,5,7,9,11,13,15},{16,18,20,22,24,26,28,30},{17..., dimensions={0} | all-to-all | bytes 393216 | tf_op jit(solution)/shard_map/all_to_all | solution.py:27
  236.4 10.0 %all_to_all.22 = bf16[8,6,768]{2,1,0:T(8,128)(2,1)S(1)} all-to-all(bf16[8,6,768]{2,1,0:T(8,128)(2,1)S(1)} %broadcast_in_dim.38), channel_id=1, replica_groups={{0,2,4,6,8,10,12,14},{1,3,5,7,9,11,13,15},{16,18,20,22,24,26,28,30},{17..., dimensions={0} | all-to-all | bytes 147456 | tf_op jit(solution)/shard_map/all_to_all | solution.py:27
  246.5 18.0 %all_to_all.23 = bf16[16,48,768]{2,1,0:T(8,128)(2,1)} all-to-all(bf16[16,48,768]{2,1,0:T(8,128)(2,1)S(1)} %broadcast_in_dim.40), channel_id=1, replica_groups={{0,16,32,48,64,80,96,112,128,144,160,176,192,208,224,240},{1,17,33,49,6..., dimensions={0} | all-to-all | bytes 2359296 | tf_op jit(solution)/shard_map/all_to_all | solution.py:27
  264.4 5.3 %collective-permute-start.123 = (bf16[768,768]{1,0:T(8,128)(2,1)}, bf16[768,768]{1,0:T(8,128)(2,1)}, u32[]{:S(2)}, u32[]{:S(2)}) collective-permute-start(bf16[768,768]{1,0:T(8,128)(2,1)} %bitcast.10), channel_id=1, source_target_pairs={{0,1},{1,0},{2,3},{3,2},{4,5},{5,4},{6,7},{7,6},{8,9},{9,8},{10,11... | collective-permute-start | bytes 3538952 | tf_op jit(solution)/shard_map/ppermute | solution.py:23
  269.8 1.2 convolution_convert_fusion
  271.0 1.3 convolution_convert_fusion.1
  272.8 4.1 %select_convert_fusion = (f32[768,768]{1,0:T(8,128)}, f32[768,768]{1,0:T(8,128)}) fusion(bf16[768,768]{1,0:T(8,128)(2,1)} %collective-permute-done.123, pred[]{:T(512)S(6)} %eq.9, bf16[16,48,768]{2,1,0:T(8,128)(2,1)} %all_to_all.23), kind=kLoop, calls=%fused_computation.5 | loop fusion | flops 2359296 | bytes 7077889 | tf_op jit(solution)/shard_map/convert_element_type | solution.py:223
  (59 shorter events, 9.8 us)
Async XLA Ops:
  0.6 1.3 copy-start
  1.9 1.3 copy-start.2
  3.2 1.0 copy-start.4
  4.2 1.0 copy-start.6
  5.2 18.3 %copy-start.12 = (s32[4]{0:T(128)S(1)}, s32[4]{0:T(128)}, u32[]{:S(2)}) copy-start(s32[4]{0:T(128)} %param.81) | copy-start | bytes 52
  7.2 0.7 copy-start.10
  7.9 166.4 %collective-permute-start.120 = (bf16[512,768]{1,0:T(8,128)(2,1)}, bf16[512,768]{1,0:T(8,128)(2,1)S(1)}, u32[]{:S(2)}, u32[]{:S(2)}) collective-permute-start(bf16[512,768]{1,0:T(8,128)(2,1)} %get-tuple-element.424), channel_id=1, source_target_pairs={{0,255},{1,0},{2,1},{3,2},{4,3},{5,4},{6,5},{7,6},{8,7},{9,8},{10,... | collective-permute-start | bytes 2359304 | tf_op jit(solution)/shard_map/ppermute | solution.py:19
  21.7 152.6 %collective-permute-start.121 = (bf16[512,768]{1,0:T(8,128)(2,1)}, bf16[512,768]{1,0:T(8,128)(2,1)}, u32[]{:S(2)}, u32[]{:S(2)}) collective-permute-start(bf16[512,768]{1,0:T(8,128)(2,1)} %get-tuple-element.424), channel_id=1, source_target_pairs={{0,1},{1,2},{2,3},{3,4},{4,5},{5,6},{6,7},{7,8},{8,9},{9,10},{10,1... | collective-permute-start | bytes 2359304 | tf_op jit(solution)/shard_map/ppermute | solution.py:19
  26.2 39.9 %collective-permute-start.64 = (bf16[256,768]{1,0:T(8,128)(2,1)}, bf16[256,768]{1,0:T(8,128)(2,1)}, u32[]{:S(2)}, u32[]{:S(2)}) collective-permute-start(bf16[256,768]{1,0:T(8,128)(2,1)} %get-tuple-element.345), channel_id=1, source_target_pairs={{0,6},{1,7},{2,8},{3,9},{4,10},{5,11},{6,12},{7,13},{8,14},{9,15},... | collective-permute-start | bytes 1179656 | tf_op jit(solution)/shard_map/cond/branch_2_fun/ppermute | solution.py:19
  31.3 34.9 %collective-permute-start.65 = (bf16[256,768]{1,0:T(8,128)(2,1)}, bf16[256,768]{1,0:T(8,128)(2,1)}, u32[]{:S(2)}, u32[]{:S(2)}) collective-permute-start(bf16[256,768]{1,0:T(8,128)(2,1)} %get-tuple-element.346), channel_id=1, source_target_pairs={{0,250},{1,251},{2,252},{3,253},{4,254},{5,255},{6,0},{7,1},{8,2},... | collective-permute-start | bytes 1179656 | tf_op jit(solution)/shard_map/cond/branch_2_fun/ppermute | solution.py:19
  77.9 28.5 %collective-permute-start.26 = (bf16[256,768]{1,0:T(8,128)(2,1)}, bf16[256,768]{1,0:T(8,128)(2,1)}, u32[]{:S(2)}, u32[]{:S(2)}) collective-permute-start(bf16[256,768]{1,0:T(8,128)(2,1)} %get-tuple-element.307), channel_id=1, source_target_pairs={{0,250},{1,251},{2,252},{3,253},{4,254},{5,255},{6,0},{7,1},{8,2},... | collective-permute-start | bytes 1179656 | tf_op jit(solution)/shard_map/cond/branch_14_fun/ppermute | solution.py:19
  82.3 28.7 %collective-permute-start.27 = (bf16[256,768]{1,0:T(8,128)(2,1)}, bf16[256,768]{1,0:T(8,128)(2,1)}, u32[]{:S(2)}, u32[]{:S(2)}) collective-permute-start(bf16[256,768]{1,0:T(8,128)(2,1)} %get-tuple-element.308), channel_id=1, source_target_pairs={{0,6},{1,7},{2,8},{3,9},{4,10},{5,11},{6,12},{7,13},{8,14},{9,15},... | collective-permute-start | bytes 1179656 | tf_op jit(solution)/shard_map/cond/branch_14_fun/ppermute | solution.py:19
  121.8 14.4 %collective-permute-start.108 = (bf16[256,768]{1,0:T(8,128)(2,1)}, bf16[256,768]{1,0:T(8,128)(2,1)S(1)}, u32[]{:S(2)}, u32[]{:S(2)}) collective-permute-start(bf16[256,768]{1,0:T(8,128)(2,1)} %get-tuple-element.389), channel_id=1, source_target_pairs={{0,96},{1,97},{2,98},{3,99},{4,100},{5,101},{6,102},{7,103},{8,104... | collective-permute-start | bytes 1179656 | tf_op jit(solution)/shard_map/cond/branch_10_fun/ppermute | solution.py:19
  121.9 22.8 %collective-permute-start.109 = (bf16[256,768]{1,0:T(8,128)(2,1)}, bf16[256,768]{1,0:T(8,128)(2,1)S(1)}, u32[]{:S(2)}, u32[]{:S(2)}) collective-permute-start(bf16[256,768]{1,0:T(8,128)(2,1)} %get-tuple-element.390), channel_id=1, source_target_pairs={{0,160},{1,161},{2,162},{3,163},{4,164},{5,165},{6,166},{7,167},{8... | collective-permute-start | bytes 1179656 | tf_op jit(solution)/shard_map/cond/branch_10_fun/ppermute | solution.py:19
  145.4 28.9 %copy-start.5 = (bf16[256,768]{1,0:T(8,128)(2,1)S(1)}, bf16[256,768]{1,0:T(8,128)(2,1)}, u32[]{:S(2)}) copy-start(bf16[256,768]{1,0:T(8,128)(2,1)} %xi_ref.3) | copy-start | bytes 1179652
  145.4 28.9 %copy-start.7 = (bf16[256,768]{1,0:T(8,128)(2,1)S(1)}, bf16[256,768]{1,0:T(8,128)(2,1)}, u32[]{:S(2)}) copy-start(bf16[256,768]{1,0:T(8,128)(2,1)} %xt_ref.3) | copy-start | bytes 1179652
  150.4 10.5 %collective-permute-start.38 = (bf16[256,768]{1,0:T(8,128)(2,1)}, bf16[256,768]{1,0:T(8,128)(2,1)S(1)}, u32[]{:S(2)}, u32[]{:S(2)}) collective-permute-start(bf16[256,768]{1,0:T(8,128)(2,1)} %get-tuple-element.319), channel_id=1, source_target_pairs={{0,176},{1,177},{2,178},{3,179},{4,180},{5,181},{6,182},{7,183},{8... | collective-permute-start | bytes 1179656 | tf_op jit(solution)/shard_map/cond/branch_5_fun/ppermute | solution.py:19
  150.5 16.2 %collective-permute-start.39 = (bf16[256,768]{1,0:T(8,128)(2,1)}, bf16[256,768]{1,0:T(8,128)(2,1)S(1)}, u32[]{:S(2)}, u32[]{:S(2)}) collective-permute-start(bf16[256,768]{1,0:T(8,128)(2,1)} %get-tuple-element.320), channel_id=1, source_target_pairs={{0,80},{1,81},{2,82},{3,83},{4,84},{5,85},{6,86},{7,87},{8,88},{9,... | collective-permute-start | bytes 1179656 | tf_op jit(solution)/shard_map/cond/branch_5_fun/ppermute | solution.py:19
  174.3 1.0 copy-start.11
  182.0 6.5 %copy-start.8 = (bf16[256,768]{1,0:T(8,128)(2,1)}, bf16[256,768]{1,0:T(8,128)(2,1)S(1)}, u32[]{:S(2)}) copy-start(bf16[256,768]{1,0:T(8,128)(2,1)S(1)} %get-tuple-element.431) | copy-start | bytes 1179652
  182.0 6.2 %collective-permute-start.122 = (f32[776,768]{1,0:T(8,128)S(1)}, f32[776,768]{1,0:T(8,128)S(1)}, u32[]{:S(2)}, u32[]{:S(2)}) collective-permute-start(f32[776,768]{1,0:T(8,128)S(1)} %get-tuple-element.433), channel_id=1, source_target_pairs={{0,1},{1,0},{2,3},{3,2},{4,5},{5,4},{6,7},{7,6},{8,9},{9,8},{10,11... | collective-permute-start | bytes 7151624 | tf_op jit(solution)/shard_map/ppermute | solution.py:23
  246.4 23.3 %copy-start.1 = (bf16[768,768]{1,0:T(8,128)(2,1)S(1)}, bf16[768,768]{1,0:T(8,128)(2,1)}, u32[]{:S(2)}) copy-start(bf16[768,768]{1,0:T(8,128)(2,1)} %wt_ref.1) | copy-start | bytes 3538948
  246.5 23.3 %copy-start.9 = (bf16[256,768]{1,0:T(8,128)(2,1)S(1)}, bf16[256,768]{1,0:T(8,128)(2,1)}, u32[]{:S(2)}) copy-start(bf16[256,768]{1,0:T(8,128)(2,1)} %copy-done.8) | copy-start | bytes 1179652
  264.4 6.6 %copy-start.3 = (bf16[768,768]{1,0:T(8,128)(2,1)S(1)}, bf16[768,768]{1,0:T(8,128)(2,1)}, u32[]{:S(2)}) copy-start(bf16[768,768]{1,0:T(8,128)(2,1)} %wi_ref.1) | copy-start | bytes 3538948
  264.4 8.3 %collective-permute-start.123 = (bf16[768,768]{1,0:T(8,128)(2,1)}, bf16[768,768]{1,0:T(8,128)(2,1)}, u32[]{:S(2)}, u32[]{:S(2)}) collective-permute-start(bf16[768,768]{1,0:T(8,128)(2,1)} %bitcast.10), channel_id=1, source_target_pairs={{0,1},{1,0},{2,3},{3,2},{4,5},{5,4},{6,7},{7,6},{8,9},{9,8},{10,11... | collective-permute-start | bytes 3538952 | tf_op jit(solution)/shard_map/ppermute | solution.py:23
